TPU v7x, 32 devices: a whole 2x2x4 slice. The times are simulated.
32 devices in a mesh: views: 8 (over y, x, core), slab: 4 (over z).
Axes of the slice: x: 2, y: 2, z: 4, core: 2. Of those that a mesh axis runs over, the one named last changes fastest.
Arguments:
- view_blocks: bfloat16 [8, 64, 64, 4096], P('views', 'slab'), may hold values from -6 to 6
- shifts: int32 [3, 8], replicated, may hold values from -512 to 512
- taps: float32 [3, 8, 4], replicated, may hold values from 0.1 to 0.7
- ztaps: float32 [3, 8, 3], replicated, may hold values from 0.15 to 0.6
Outputs:
- merged: bfloat16 [8, 64, 8, 4096], P('views', 'slab')
All inputs are finite; a program needn't handle non-finite values.
Results may differ from a plain program's by a relative error of at most 0.0058.
Values may be sent and summed in bfloat16 or wider, within the bound.
A program may use at most 128 MiB of HBM per device.

v0:
```python
import jax
import jax.numpy as jnp
from jax import lax
from jax.sharding import PartitionSpec as P

LEVELS = 3


def extended(cells, sides, width):
    for axis, dim in sides:
        count = lax.axis_size(axis)
        ends = count - 1
        head = lax.slice_in_dim(cells, 0, width, axis=dim)
        tail = lax.slice_in_dim(cells, cells.shape[dim] - width, cells.shape[dim], axis=dim)
        cells = jnp.concatenate(
            [
                lax.ppermute(tail, axis, [(i, (i + 1) % count) for i in range(ends)]),
                cells,
                lax.ppermute(head, axis, [((i + 1) % count, i) for i in range(ends)]),
            ],
            axis=dim,
        )
    return cells


def swapped(value, axis, distance):
    mask = 2**distance
    pairs = [(source, source ^ mask) for source in range(lax.axis_size(axis))]
    return lax.ppermute(value, axis, pairs)


def transform(padded, zweights, cweights, shift):
    zmix = zweights[0] * padded[:, :-2].astype(jnp.float32)
    zmix = zmix + zweights[1] * padded[:, 1:-1].astype(jnp.float32)
    zmix = zmix + zweights[2] * padded[:, 2:].astype(jnp.float32)
    width = zmix.shape[3]
    margin = width // 8 + 2
    wide = jnp.pad(zmix, ((0, 0), (0, 0), (0, 0), (margin, margin)))
    total = jnp.zeros(zmix.shape, jnp.float32)
    for tap_index in range(cweights.shape[0]):
        start = margin + shift + tap_index - 1
        total = total + cweights[tap_index] * lax.dynamic_slice_in_dim(wide, start, width, 3)
    return total.astype(jnp.bfloat16)


def shards(view_blocks, shifts, taps, ztaps):
    position = lax.axis_index("views")
    block = view_blocks
    for level in range(LEVELS):
        group = position >> level
        upper = group & 1
        rows = block.shape[2]
        half = rows // 2
        keep_start = upper * half
        send_start = (1 - upper) * half
        padded = extended(block, (("slab", 1),), 1)
        interp = transform(padded, ztaps[level][group], taps[level][group], shifts[level][group])
        kept = lax.dynamic_slice_in_dim(interp, keep_start, half, 2)
        sent = lax.dynamic_slice_in_dim(interp, send_start, half, 2)
        received = swapped(sent, "views", level)
        block = (0.5 * (kept.astype(jnp.float32) + received.astype(jnp.float32))).astype(
            jnp.bfloat16
        )
    return block


def solution(mesh):
    return jax.shard_map(
        shards,
        mesh=mesh,
        in_specs=(P("views", "slab", None, None), P(), P(), P()),
        out_specs=P("views", "slab", None, None),
        check_vma=False,
    )
```

profile of v0, /device:TPU:0, one launch (start us, length us, event | category | flops | bytes accessed | tf_op | source)
XLA Modules:
  0.0 227.7 jit_solution(14056028723860333327)
XLA Ops:
  0.0 1.3 fusion.24
  1.3 5.0 %collective-permute-start = (bf16[1,1,64,4096]{3,2,1,0:T(8,128)(2,1)S(1)}, bf16[1,1,64,4096]{3,2,1,0:T(8,128)(2,1)S(1)}, u32[]{:S(2)}, u32[]{:S(2)}) collective-permute-start(bf16[1,1,64,4096]{3,2,1,0:T(8,128)(2,1)S(1)} %get-tuple-element.5), channel_id=1, source_target_pairs={{0,1},{1,2},{2,3},{4,5},{5,6},{6,7},{8,9},{9,10},{10,11},{12,13},{... | collective-permute-start | bytes 1572872 | tf_op jit(solution)/shard_map/ppermute | solution.py:17
  6.2 1.3 collective-permute-start.1
  7.5 0.8 fusion.35
  8.3 0.7 fusion.36
  14.4 0.7 fusion.28
  15.8 0.1 constant_dynamic-slice_fusion.6
  15.8 0.7 fusion.27
  16.6 0.1 constant_dynamic-slice_fusion.7
  16.6 0.5 fusion.34
  17.2 0.6 fusion.33
  17.8 0.0 collective-permute-done
  17.8 3.7 %collective-permute-done.1 = bf16[1,1,64,4096]{3,2,1,0:T(8,128)(2,1)S(1)} collective-permute-done((bf16[1,1,64,4096]{3,2,1,0:T(8,128)(2,1)S(1)}, bf16[1,1,64,4096]{3,2,1,0:T(8,128)(2,1)S(1)}, u32[]{:S(2)}, u32[]{:S(2)}) %collective-permute-start.1) | collective-permute-done | bytes 524320 | tf_op jit(solution)/shard_map/ppermute | solution.py:19
  21.5 16.6 %multiply_add_fusion = f32[1,16,64,4096]{3,2,1,0:T(8,128)} fusion(bf16[1,16,64,4096]{3,2,1,0:T(8,128)(2,1)} %param.4, bf16[1,1,64,4096]{3,2,1,0:T(8,128)(2,1)S(1)} %collective-permute-done.1, bf16[1,1,64,4096]{3,2,1,0:T(8,128)(2,1)S(1)} %collective-permute-done, f32[]{:T(128)} %bitcast.7, f32[]{:T(128)} %bitcast.6, f32[]{:T(128)} %bitcast.5), kind=kLoop, calls=%fused_computation.12 | loop fusion | flops 41943040 | bytes 26214412 | tf_op jit(solution)/shard_map/add | solution.py:35
  38.1 27.5 %fusion.4 = bf16[1,16,64,4096]{3,2,1,0:T(8,128)(2,1)S(1)} fusion(s32[]{:T(128)S(6)} %select_n.72, f32[1,16,64,4096]{3,2,1,0:T(8,128)} %multiply_add_fusion, s32[]{:T(128)S(6)} %select_n.73, s32[]{:T(128)S(6)} %select_n.74, s32[]{:T(128)S(6)} %select_n.75, f32[]{:T(128)} %bitcast.16, f32[]{:T(128)} %bitcast.13, f32[]{:T(128)} %bitcast.10, f32[]{:T(128)} %bitcast.4), kind=kLoop, calls=%fused_computation.8 | loop fusion | flops 33554432 | bytes 25165856 | tf_op jit(solution)/shard_map/convert_element_type | solution.py:43
  65.6 0.0 copy-start
  65.6 3.3 %copy-done = bf16[1,16,64,4096]{3,2,1,0:T(8,128)(2,1)} copy-done((bf16[1,16,64,4096]{3,2,1,0:T(8,128)(2,1)}, bf16[1,16,64,4096]{3,2,1,0:T(8,128)(2,1)S(1)}, u32[]{:S(2)}) %copy-start) | copy-done | bytes 8388632
  68.9 2.4 %constant_dynamic-slice_fusion.3 = bf16[1,16,32,4096]{3,2,1,0:T(8,128)(2,1)} fusion(bf16[1,16,64,4096]{3,2,1,0:T(8,128)(2,1)S(1)} %fusion.4, s32[]{:T(128)S(6)} %select_n.77), kind=kLoop, calls=%fused_computation.51 | loop fusion | bytes 8388612 | tf_op jit(solution)/shard_map/dynamic_slice | solution.py:59
  71.3 0.0 collective-permute-start.2
  71.3 7.5 %collective-permute-done.2 = bf16[1,16,32,4096]{3,2,1,0:T(8,128)(2,1)} collective-permute-done((bf16[1,16,32,4096]{3,2,1,0:T(8,128)(2,1)}, bf16[1,16,32,4096]{3,2,1,0:T(8,128)(2,1)}, u32[]{:S(2)}, u32[]{:S(2)}) %collective-permute-start.2) | collective-permute-done | bytes 4194336 | tf_op jit(solution)/shard_map/ppermute | solution.py:29
  78.8 4.9 %multiply_convert_fusion = bf16[1,16,32,4096]{3,2,1,0:T(8,128)(2,1)S(1)} fusion(bf16[1,16,32,4096]{3,2,1,0:T(8,128)(2,1)} %collective-permute-done.2, bf16[1,16,64,4096]{3,2,1,0:T(8,128)(2,1)} %copy-done, s32[]{:T(128)S(6)} %select_n.76), kind=kLoop, calls=%fused_computation.28 | loop fusion | flops 10485760 | bytes 12582916 | tf_op jit(solution)/shard_map/convert_element_type | solution.py:61
  83.7 0.0 copy-start.1
  83.8 1.9 copy-done.1
  85.7 3.5 %collective-permute-start.3 = (bf16[1,1,32,4096]{3,2,1,0:T(8,128)(2,1)S(1)}, bf16[1,1,32,4096]{3,2,1,0:T(8,128)(2,1)S(1)}, u32[]{:S(2)}, u32[]{:S(2)}) collective-permute-start(bf16[1,1,32,4096]{3,2,1,0:T(8,128)(2,1)S(1)} %get-tuple-element.7), channel_id=1, source_target_pairs={{0,1},{1,2},{2,3},{4,5},{5,6},{6,7},{8,9},{9,10},{10,11},{12,13},{... | collective-permute-start | bytes 786440 | tf_op jit(solution)/shard_map/ppermute | solution.py:17
  89.2 1.5 collective-permute-start.4
  96.1 0.6 fusion.32
  96.7 0.6 fusion.31
  97.3 0.0 collective-permute-done.3
  97.3 1.9 collective-permute-done.4
  99.2 7.8 %multiply_add_fusion.1 = f32[1,16,32,4096]{3,2,1,0:T(8,128)S(1)} fusion(bf16[1,16,32,4096]{3,2,1,0:T(8,128)(2,1)} %copy-done.1, bf16[1,1,32,4096]{3,2,1,0:T(8,128)(2,1)S(1)} %collective-permute-done.4, bf16[1,1,32,4096]{3,2,1,0:T(8,128)(2,1)S(1)} %collective-permute-done.3, f32[]{:T(128)} %bitcast.20, f32[]{:T(128)} %bitcast.19, f32[]{:T(128)} %bitcast.3), kind=kLoop, calls=%fused_computation.27 | loop fusion | flops 20971520 | bytes 13107212 | tf_op jit(solution)/shard_map/add | solution.py:35
  107.0 11.3 %fusion.12 = bf16[1,16,32,4096]{3,2,1,0:T(8,128)(2,1)S(1)} fusion(s32[]{:T(128)S(6)} %select_n.78, f32[1,16,32,4096]{3,2,1,0:T(8,128)S(1)} %multiply_add_fusion.1, s32[]{:T(128)S(6)} %select_n.79, s32[]{:T(128)S(6)} %select_n.80, s32[]{:T(128)S(6)} %select_n.81, f32[]{:T(128)} %bitcast.29, f32[]{:T(128)} %bitcast.26, f32[]{:T(128)} %bitcast.23, f32[]{:T(128)} %bitcast.2), kind=kLoop, calls=%fused_computation.21 | loop fusion | flops 16777216 | bytes 12582944 | tf_op jit(solution)/shard_map/convert_element_type | solution.py:43
  118.3 0.0 copy-start.2
  118.3 1.9 copy-done.2
  120.2 1.6 constant_dynamic-slice_fusion.1
  121.9 1.5 collective-permute-start.5
  123.3 0.1 constant_dynamic-slice_fusion.10
  123.4 0.6 fusion.30
  124.0 44.7 %collective-permute-done.5 = bf16[1,16,16,4096]{3,2,1,0:T(8,128)(2,1)} collective-permute-done((bf16[1,16,16,4096]{3,2,1,0:T(8,128)(2,1)}, bf16[1,16,16,4096]{3,2,1,0:T(8,128)(2,1)}, u32[]{:S(2)}, u32[]{:S(2)}) %collective-permute-start.5) | collective-permute-done | bytes 2097184 | tf_op jit(solution)/shard_map/ppermute | solution.py:29
  168.7 3.0 %multiply_convert_fusion.1 = bf16[1,16,16,4096]{3,2,1,0:T(8,128)(2,1)S(1)} fusion(bf16[1,16,16,4096]{3,2,1,0:T(8,128)(2,1)} %collective-permute-done.5, bf16[1,16,32,4096]{3,2,1,0:T(8,128)(2,1)} %copy-done.2, s32[]{:T(128)S(6)} %select_n.82), kind=kLoop, calls=%fused_computation.44 | loop fusion | flops 5242880 | bytes 6291460 | tf_op jit(solution)/shard_map/convert_element_type | solution.py:61
  171.7 3.5 %collective-permute-start.6 = (bf16[1,1,16,4096]{3,2,1,0:T(8,128)(2,1)S(1)}, bf16[1,1,16,4096]{3,2,1,0:T(8,128)(2,1)S(1)}, u32[]{:S(2)}, u32[]{:S(2)}) collective-permute-start(bf16[1,1,16,4096]{3,2,1,0:T(8,128)(2,1)S(1)} %get-tuple-element.9), channel_id=1, source_target_pairs={{0,1},{1,2},{2,3},{4,5},{5,6},{6,7},{8,9},{9,10},{10,11},{12,13},{... | collective-permute-start | bytes 393224 | tf_op jit(solution)/shard_map/ppermute | solution.py:17
  175.2 1.5 collective-permute-start.7
  176.7 0.1 constant_dynamic-slice_fusion.11
  176.8 0.6 fusion.38
  183.4 0.6 fusion.29
  184.0 0.0 collective-permute-done.6
  184.1 0.0 collective-permute-done.7
  184.1 3.1 %multiply_add_fusion.2 = f32[1,16,16,4096]{3,2,1,0:T(8,128)S(1)} fusion(bf16[1,16,16,4096]{3,2,1,0:T(8,128)(2,1)S(1)} %multiply_convert_fusion.1, bf16[1,1,16,4096]{3,2,1,0:T(8,128)(2,1)S(1)} %collective-permute-done.7, bf16[1,1,16,4096]{3,2,1,0:T(8,128)(2,1)S(1)} %collective-permute-done.6, f32[]{:T(128)} %bitcast.33, f32[]{:T(128)} %bitcast.32, f32[]{:T(128)} %bitcast.1), kind=kLoop, calls=%fused_computation.43 | loop fusion | flops 10485760 | bytes 6553612 | tf_op jit(solution)/shard_map/add | solution.py:35
  187.2 7.1 %fusion.20 = bf16[1,16,16,4096]{3,2,1,0:T(8,128)(2,1)S(1)} fusion(s32[]{:T(128)S(6)} %select_n.84, f32[1,16,16,4096]{3,2,1,0:T(8,128)S(1)} %multiply_add_fusion.2, s32[]{:T(128)S(6)} %select_n.85, s32[]{:T(128)S(6)} %select_n.86, s32[]{:T(128)S(6)} %select_n.87, f32[]{:T(128)} %bitcast.42, f32[]{:T(128)} %bitcast.39, f32[]{:T(128)} %bitcast.36, f32[]{:T(128)} %bitcast), kind=kLoop, calls=%fused_computation.37 | loop fusion | flops 8388608 | bytes 6291488 | tf_op jit(solution)/shard_map/convert_element_type | solution.py:43
  194.2 0.1 constant_dynamic-slice_fusion.4
  194.4 9.4 %collective-permute-start.8 = (bf16[1,16,8,4096]{3,2,1,0:T(8,128)(2,1)S(1)}, bf16[1,16,8,4096]{3,2,1,0:T(8,128)(2,1)}, u32[]{:S(2)}, u32[]{:S(2)}) collective-permute-start(bf16[1,16,8,4096]{3,2,1,0:T(8,128)(2,1)S(1)} %constant_dynamic-slice_fusion.4), channel_id=1, source_target_pairs={{0,16},{4,20},{8,24},{12,28},{16,0},{20,4},{24,8},{28,12},{1,17},{... | collective-permute-start | bytes 3145736 | tf_op jit(solution)/shard_map/ppermute | solution.py:29
  203.8 21.5 %collective-permute-done.8 = bf16[1,16,8,4096]{3,2,1,0:T(8,128)(2,1)} collective-permute-done((bf16[1,16,8,4096]{3,2,1,0:T(8,128)(2,1)S(1)}, bf16[1,16,8,4096]{3,2,1,0:T(8,128)(2,1)}, u32[]{:S(2)}, u32[]{:S(2)}) %collective-permute-start.8) | collective-permute-done | bytes 1048608 | tf_op jit(solution)/shard_map/ppermute | solution.py:29
  225.2 2.5 %multiply_convert_fusion.2 = bf16[1,16,8,4096]{3,2,1,0:T(8,128)(2,1)} fusion(bf16[1,16,8,4096]{3,2,1,0:T(8,128)(2,1)} %collective-permute-done.8, bf16[1,16,16,4096]{3,2,1,0:T(8,128)(2,1)S(1)} %fusion.20, s32[]{:T(128)S(6)} %select_n.88), kind=kLoop, calls=%fused_computation.47 | loop fusion | flops 2621440 | bytes 3145732 | tf_op jit(solution)/shard_map/convert_element_type | solution.py:61
  (2 shorter events, 0.1 us)
Async XLA Ops:
  1.3 16.5 %collective-permute-start = (bf16[1,1,64,4096]{3,2,1,0:T(8,128)(2,1)S(1)}, bf16[1,1,64,4096]{3,2,1,0:T(8,128)(2,1)S(1)}, u32[]{:S(2)}, u32[]{:S(2)}) collective-permute-start(bf16[1,1,64,4096]{3,2,1,0:T(8,128)(2,1)S(1)} %get-tuple-element.5), channel_id=1, source_target_pairs={{0,1},{1,2},{2,3},{4,5},{5,6},{6,7},{8,9},{9,10},{10,11},{12,13},{... | collective-permute-start | bytes 1572872 | tf_op jit(solution)/shard_map/ppermute | solution.py:17
  6.2 15.3 %collective-permute-start.1 = (bf16[1,1,64,4096]{3,2,1,0:T(8,128)(2,1)S(1)}, bf16[1,1,64,4096]{3,2,1,0:T(8,128)(2,1)S(1)}, u32[]{:S(2)}, u32[]{:S(2)}) collective-permute-start(bf16[1,1,64,4096]{3,2,1,0:T(8,128)(2,1)S(1)} %get-tuple-element.6), channel_id=1, source_target_pairs={{1,0},{2,1},{3,2},{5,4},{6,5},{7,6},{9,8},{10,9},{11,10},{13,12},{... | collective-permute-start | bytes 1572872 | tf_op jit(solution)/shard_map/ppermute | solution.py:19
  65.6 3.3 %copy-start = (bf16[1,16,64,4096]{3,2,1,0:T(8,128)(2,1)}, bf16[1,16,64,4096]{3,2,1,0:T(8,128)(2,1)S(1)}, u32[]{:S(2)}) copy-start(bf16[1,16,64,4096]{3,2,1,0:T(8,128)(2,1)S(1)} %fusion.4) | copy-start | bytes 25165828
  71.3 7.5 %collective-permute-start.2 = (bf16[1,16,32,4096]{3,2,1,0:T(8,128)(2,1)}, bf16[1,16,32,4096]{3,2,1,0:T(8,128)(2,1)}, u32[]{:S(2)}, u32[]{:S(2)}) collective-permute-start(bf16[1,16,32,4096]{3,2,1,0:T(8,128)(2,1)} %constant_dynamic-slice_fusion.3), channel_id=1, source_target_pairs={{0,4},{4,0},{8,12},{12,8},{16,20},{20,16},{24,28},{28,24},{1,5},{5... | collective-permute-start | bytes 12582920 | tf_op jit(solution)/shard_map/ppermute | solution.py:29
  83.7 2.0 copy-start.1
  85.7 11.5 %collective-permute-start.3 = (bf16[1,1,32,4096]{3,2,1,0:T(8,128)(2,1)S(1)}, bf16[1,1,32,4096]{3,2,1,0:T(8,128)(2,1)S(1)}, u32[]{:S(2)}, u32[]{:S(2)}) collective-permute-start(bf16[1,1,32,4096]{3,2,1,0:T(8,128)(2,1)S(1)} %get-tuple-element.7), channel_id=1, source_target_pairs={{0,1},{1,2},{2,3},{4,5},{5,6},{6,7},{8,9},{9,10},{10,11},{12,13},{... | collective-permute-start | bytes 786440 | tf_op jit(solution)/shard_map/ppermute | solution.py:17
  89.2 10.0 %collective-permute-start.4 = (bf16[1,1,32,4096]{3,2,1,0:T(8,128)(2,1)S(1)}, bf16[1,1,32,4096]{3,2,1,0:T(8,128)(2,1)S(1)}, u32[]{:S(2)}, u32[]{:S(2)}) collective-permute-start(bf16[1,1,32,4096]{3,2,1,0:T(8,128)(2,1)S(1)} %get-tuple-element.8), channel_id=1, source_target_pairs={{1,0},{2,1},{3,2},{5,4},{6,5},{7,6},{9,8},{10,9},{11,10},{13,12},{... | collective-permute-start | bytes 786440 | tf_op jit(solution)/shard_map/ppermute | solution.py:19
  118.3 2.0 copy-start.2
  121.9 46.8 %collective-permute-start.5 = (bf16[1,16,16,4096]{3,2,1,0:T(8,128)(2,1)}, bf16[1,16,16,4096]{3,2,1,0:T(8,128)(2,1)}, u32[]{:S(2)}, u32[]{:S(2)}) collective-permute-start(bf16[1,16,16,4096]{3,2,1,0:T(8,128)(2,1)} %constant_dynamic-slice_fusion.1), channel_id=1, source_target_pairs={{0,8},{4,12},{8,0},{12,4},{16,24},{20,28},{24,16},{28,20},{1,9},{5... | collective-permute-start | bytes 6291464 | tf_op jit(solution)/shard_map/ppermute | solution.py:29
  171.7 12.4 %collective-permute-start.6 = (bf16[1,1,16,4096]{3,2,1,0:T(8,128)(2,1)S(1)}, bf16[1,1,16,4096]{3,2,1,0:T(8,128)(2,1)S(1)}, u32[]{:S(2)}, u32[]{:S(2)}) collective-permute-start(bf16[1,1,16,4096]{3,2,1,0:T(8,128)(2,1)S(1)} %get-tuple-element.9), channel_id=1, source_target_pairs={{0,1},{1,2},{2,3},{4,5},{5,6},{6,7},{8,9},{9,10},{10,11},{12,13},{... | collective-permute-start | bytes 393224 | tf_op jit(solution)/shard_map/ppermute | solution.py:17
  175.2 8.9 %collective-permute-start.7 = (bf16[1,1,16,4096]{3,2,1,0:T(8,128)(2,1)S(1)}, bf16[1,1,16,4096]{3,2,1,0:T(8,128)(2,1)S(1)}, u32[]{:S(2)}, u32[]{:S(2)}) collective-permute-start(bf16[1,1,16,4096]{3,2,1,0:T(8,128)(2,1)S(1)} %get-tuple-element.10), channel_id=1, source_target_pairs={{1,0},{2,1},{3,2},{5,4},{6,5},{7,6},{9,8},{10,9},{11,10},{13,12},{... | collective-permute-start | bytes 393224 | tf_op jit(solution)/shard_map/ppermute | solution.py:19
  194.4 30.9 %collective-permute-start.8 = (bf16[1,16,8,4096]{3,2,1,0:T(8,128)(2,1)S(1)}, bf16[1,16,8,4096]{3,2,1,0:T(8,128)(2,1)}, u32[]{:S(2)}, u32[]{:S(2)}) collective-permute-start(bf16[1,16,8,4096]{3,2,1,0:T(8,128)(2,1)S(1)} %constant_dynamic-slice_fusion.4), channel_id=1, source_target_pairs={{0,16},{4,20},{8,24},{12,28},{16,0},{20,4},{24,8},{28,12},{1,17},{... | collective-permute-start | bytes 3145736 | tf_op jit(solution)/shard_map/ppermute | solution.py:29
where the time goes:
time: 229 us; the launch traced here: 228 us
  other arithmetic  85.1 us (37%)
  waiting for transfers between devices  79.3 us (35%)
  starting transfers between devices  27.1 us (12%)
  local copies, waits for them, and re-layouts  18.7 us (8%)
  between operations  17.6 us (8%)
    ppermute x3, waiting for transfers between devices, swapped(): return lax.ppermute(value, axis, pairs)  73.6 us
    convert_element_type x3, other arithmetic, transform(): return total.astype(jnp.bfloat16)  45.8 us
    add x3, other arithmetic, transform(): zmix = zmix + zweights[2] * padded[:, 2:].astype(jnp.float32)  27.5 us
    ppermute x3, starting transfers between devices, extended(): lax.ppermute(tail, axis, [(i, (i + 1) % count) for i in range(ends)])  11.9 us
    ppermute x3, starting transfers between devices, swapped(): return lax.ppermute(value, axis, pairs)  10.9 us
    convert_element_type x3, other arithmetic, shards(): (0.5 * (kept.astype(jnp.float32) + received.astype(jnp.float32))).astype(...  10.4 us
    unnamed x6, local copies, waits for them, and re-layouts  7.15 us
    ppermute x3, waiting for transfers between devices, extended(): lax.ppermute(head, axis, [((i + 1) % count, i) for i in range(ends)])  5.62 us
  transfers between devices with their start and end apart: 9, of which 5 were waited for; matrix products, arithmetic and copies ran while one was open for 3% of the time, Pallas kernels for 0%

commit v1 on v0

v1 whole, which is shorter than its diff:
```python
import functools

import jax
import jax.numpy as jnp
from jax import lax
from jax.experimental import pallas as pl
from jax.experimental.pallas import tpu as pltpu
from jax.sharding import PartitionSpec as P

LANES = 128
BLOCK = 256
WINDOW = 512
STRIP = 512
MESH = pl.DeviceIdType.MESH


def kernel(
    pairs,
    width,
    margin,
    tap_count,
    x_hbm,
    shifts,
    taps,
    ztaps,
    out,
    xin,
    h0,
    mixed0,
    mixed1,
    mixed2,
    band,
    x1,
    s0,
    r0,
    h1s,
    h1r,
    x2,
    s1,
    r1,
    h2s,
    h2r,
    k2,
    s2,
    r2,
    load_sem,
    s0_sem,
    r0_sem,
    s1_sem,
    r1_sem,
    s2_sem,
    r2_sem,
    hs_sem,
    hr_sem,
):
    view = lax.axis_index("views")
    slab = lax.axis_index("slab")
    last_slab = lax.axis_size("slab") - 1
    planes = 2 * pairs
    bit0 = view % 2
    bit1 = (view // 2) % 2
    bit2 = (view // 4) % 2
    core_peer = view + 1 - 2 * bit0
    peer1 = view + 2 - 4 * bit1
    peer2 = view + 4 - 8 * bit2
    first = bit1
    second = bit2
    below = jnp.maximum(slab - 1, 0)
    above = jnp.minimum(slab + 1, last_slab)
    has_below = slab > 0
    has_above = slab < last_slab

    loads = [
        pltpu.make_async_copy(
            x_hbm.at[pl.ds(2 * p, 2)], xin.at[pl.ds(2 * p, 2)], load_sem.at[p]
        )
        for p in range(pairs)
    ]
    order0 = [(t + 1) % pairs for t in range(pairs)]
    for p in [0] + order0[:-1]:
        loads[p].start()

    barrier = pltpu.get_barrier_semaphore()
    for peer in (core_peer, peer1, peer2):
        pl.semaphore_signal(barrier, inc=1, device_id=(peer, slab), device_id_type=MESH)

    @pl.when(has_below)
    def _():
        pl.semaphore_signal(barrier, inc=1, device_id=(view, below), device_id_type=MESH)

    @pl.when(has_above)
    def _():
        pl.semaphore_signal(barrier, inc=1, device_id=(view, above), device_id_type=MESH)

    pl.semaphore_wait(
        barrier, 3 + has_below.astype(jnp.int32) + has_above.astype(jnp.int32)
    )

    def halo(level, src_down, src_up, landing):
        down = pltpu.make_async_remote_copy(
            src_down, landing.at[1], hs_sem.at[level, 0], hr_sem.at[level, 1],
            device_id=(view, below), device_id_type=MESH,
        )
        up = pltpu.make_async_remote_copy(
            src_up, landing.at[0], hs_sem.at[level, 1], hr_sem.at[level, 0],
            device_id=(view, above), device_id_type=MESH,
        )
        return down, up

    def when_do(condition, action):
        @pl.when(condition)
        def _():
            action()

    halo0 = halo(0, x_hbm.at[0], x_hbm.at[planes - 1], h0)
    halo1 = halo(1, h1s.at[0], h1s.at[1], h1r)
    halo2 = halo(2, h2s.at[0], h2s.at[1], h2r)
    when_do(has_below, halo0[0].start)
    when_do(has_above, halo0[1].start)

    def zero_ends(landing):
        @pl.when(jnp.logical_not(has_below))
        def _():
            landing[0] = jnp.zeros(landing.shape[1:], landing.dtype)

        @pl.when(jnp.logical_not(has_above))
        def _():
            landing[1] = jnp.zeros(landing.shape[1:], landing.dtype)

    for landing in (h0, h1r, h2r):
        zero_ends(landing)

    edge_blocks = margin // LANES
    mixes = [mixed0, mixed1, mixed2]
    for mixed in mixes:
        empty = jnp.zeros((edge_blocks,) + mixed.shape[1:], mixed.dtype)
        mixed[0:edge_blocks] = empty
        mixed[mixed.shape[0] - edge_blocks :] = empty

    groups = [view, view // 2, view // 4]
    bases = []
    for level in range(3):
        start = shifts[level, groups[level]] + (margin - 1)
        base = lax.div(start, jnp.int32(LANES))
        offset = start - base * LANES
        bases.append(base)
        distance = (
            lax.broadcasted_iota(jnp.int32, (WINDOW, BLOCK), 0)
            - lax.broadcasted_iota(jnp.int32, (WINDOW, BLOCK), 1)
            - offset
        )
        values = jnp.zeros((WINDOW, BLOCK), jnp.float32)
        for k in range(tap_count):
            values = jnp.where(distance == k, 0.5 * taps[level, groups[level], k], values)
        coarse = values.astype(jnp.bfloat16)
        band[level, 0] = coarse
        band[level, 1] = (values - coarse.astype(jnp.float32)).astype(jnp.bfloat16)

    def weights(level):
        return [ztaps[level, groups[level], i] for i in range(3)]

    def strips(body):
        def step(i, carry):
            body(pl.multiple_of(i * STRIP, STRIP))
            return carry

        lax.fori_loop(0, width // STRIP, step, 0)

    def f32(value):
        return value.astype(jnp.float32)

    def put(level, row, col, lower, upper):
        value = jnp.concatenate([lower, upper], 0).astype(jnp.bfloat16)
        at = lax.div(col, LANES) + edge_blocks
        for i in range(STRIP // LANES):
            mixes[level][at + i, row : row + 16, :] = value[:, i * LANES : (i + 1) * LANES]

    def mix_first(p):
        w = weights(0)

        def body(col):
            cols = pl.ds(col, STRIP)
            for part in range(2):
                side = bit0 if part == 0 else 1 - bit0
                for i in range(2):
                    rows = pl.ds(pl.multiple_of(32 * side + 16 * i, 16), 16)
                    a = f32(h0[0, rows, cols] if p == 0 else xin[2 * p - 1, rows, cols])
                    b = f32(xin[2 * p, rows, cols])
                    c = f32(xin[2 * p + 1, rows, cols])
                    d = f32(h0[1, rows, cols] if p == pairs - 1 else xin[2 * p + 2, rows, cols])
                    lower = w[0] * a + w[1] * b + w[2] * c
                    upper = w[0] * b + w[1] * c + w[2] * d
                    put(0, 64 * part + 32 * i, col, lower[:8], upper[:8])
                    put(0, 64 * part + 32 * i + 16, col, lower[8:], upper[8:])

        strips(body)

    def mix_later(level, p, source, landing, chunk_starts):
        w = weights(level)

        def body(col):
            cols = pl.ds(col, STRIP)
            for at, chunk in enumerate(chunk_starts):
                even = at % 2 if len(chunk_starts) > 2 else None
                rows = pl.ds(pl.multiple_of(16 * chunk, 16), 16)
                here = f32(source[p, rows, cols])
                b, c = here[:8], here[8:]

                def edge(end):
                    if even is None:
                        block = f32(landing[end, 0:16, cols])
                        return jnp.where(chunk == 0, block[:8], block[8:])
                    block = f32(
                        landing[end, pl.ds(pl.multiple_of(8 * (chunk - even), 16), 16), cols]
                    )
                    return block[8 * even : 8 * even + 8]

                a = edge(0) if p == 0 else f32(source[p - 1, rows, cols])[8:]
                d = edge(1) if p == pairs - 1 else f32(source[p + 1, rows, cols])[:8]
                lower = w[0] * a + w[1] * b + w[2] * c
                upper = w[0] * b + w[1] * c + w[2] * d
                put(level, 16 * at, col, lower, upper)

        strips(body)

    def interpolate(level, p, rows, kept, sent):
        together = max(1, 512 // rows)
        base = bases[level]
        mixed = mixes[level]
        half = rows // 2

        def step(group, carry):
            windows = []
            for j in range(together):
                at = base + (BLOCK // LANES) * (group * together + j)
                windows.append(
                    jnp.concatenate([mixed[at + i] for i in range(WINDOW // LANES)], 1)
                )
            operand = jnp.concatenate(windows, 0)
            total = jnp.dot(operand, band[level, 0], preferred_element_type=jnp.float32)
            total += jnp.dot(operand, band[level, 1], preferred_element_type=jnp.float32)
            for j in range(together):
                cols = pl.ds(pl.multiple_of((group * together + j) * BLOCK, BLOCK), BLOCK)
                piece = total[j * rows : (j + 1) * rows].astype(jnp.bfloat16)
                kept[p, :, cols] = piece[:half]
                sent[p, :, cols] = piece[half:]
            return carry

        lax.fori_loop(0, width // (BLOCK * together), step, 0)

    def add_into(target, p, kept, received):
        def body(col):
            cols = pl.ds(col, STRIP)
            target[p, :, cols] = (f32(kept[p, :, cols]) + f32(received[p, :, cols])).astype(
                jnp.bfloat16
            )

        strips(body)

    def exchange(sent, received, send_sem, recv_sem, peer):
        return [
            pltpu.make_async_remote_copy(
                sent.at[p], received.at[p], send_sem.at[p], recv_sem.at[p],
                device_id=(peer, slab), device_id_type=MESH,
            )
            for p in range(pairs)
        ]

    cross0 = exchange(s0, r0, s0_sem, r0_sem, core_peer)
    cross1 = exchange(s1, r1, s1_sem, r1_sem, peer1)
    cross2 = exchange(s2, r2, s2_sem, r2_sem, peer2)

    def send_edges(p, source, ready, copies, chunks):
        for end, at, half in ((0, 0, 0), (1, pairs - 1, 8)):
            if p != at:
                continue

            def body(col):
                cols = pl.ds(col, STRIP)
                for c in range(0, chunks, 2):
                    one = f32(source[p, 16 * c : 16 * c + 16, cols])[half : half + 8]
                    two = f32(source[p, 16 * c + 16 : 16 * c + 32, cols])[half : half + 8]
                    ready[end, 8 * c : 8 * c + 16, cols] = jnp.concatenate([one, two], 0).astype(
                        jnp.bfloat16
                    )

            strips(body)
            when_do(has_below if end == 0 else has_above, copies[end].start)

    loaded = set()

    def need(p):
        if 0 <= p < pairs and p not in loaded:
            loads[p].wait()
            loaded.add(p)

    def await_halo(p, copies):
        if p == 0:
            when_do(has_below, copies[1].wait_recv)
        if p == pairs - 1:
            when_do(has_above, copies[0].wait_recv)

    def level0(p):
        for q in (p - 1, p, p + 1):
            need(q)
        await_halo(p, halo0)
        mix_first(p)
        interpolate(0, p, 128, x1, s0)
        cross0[p].start()

    def merge0(p):
        cross0[p].wait_recv()
        add_into(x1, p, x1, r0)
        send_edges(p, x1, h1s, halo1, 4)

    def level1(p):
        await_halo(p, halo1)
        own, other = 2 * first, 2 - 2 * first
        mix_later(1, p, x1, h1r, [own, own + 1, other, other + 1])
        interpolate(1, p, 64, x2, s1)
        cross1[p].start()

    def merge1(p):
        cross1[p].wait_recv()
        add_into(x2, p, x2, r1)
        send_edges(p, x2, h2s, halo2, 2)

    def level2(p):
        await_halo(p, halo2)
        mix_later(2, p, x2, h2r, [second, 1 - second])
        interpolate(2, p, 32, k2, s2)
        cross2[p].start()

    def merge2(p):
        cross2[p].wait_recv()
        add_into(out, p, k2, r2)

    for t in range(pairs + 3):
        if t < pairs:
            level0((t + 1) % pairs)
        if 1 <= t <= pairs:
            merge0(t % pairs)
        if t >= 3:
            level1((t - 1) % pairs)
    for t in range(pairs + 3):
        if t < pairs:
            merge1((t + 2) % pairs)
        if 2 <= t < pairs + 2:
            level2((t + 1) % pairs)
        if 3 <= t:
            merge2(t % pairs)

    for copies in (cross0, cross1, cross2):
        for copy in copies:
            copy.wait_send()
    for copies in (halo0, halo1, halo2):
        when_do(has_below, copies[0].wait_send)
        when_do(has_above, copies[1].wait_send)


def shards(view_blocks, shifts, taps, ztaps):
    _, planes, rows, width = view_blocks.shape
    pairs = planes // 2
    margin = width // 8 + LANES
    blocks = (width + 2 * margin) // LANES
    bf16 = jnp.bfloat16
    dma = pltpu.SemaphoreType.DMA
    vmem = pltpu.VMEM
    result = pl.pallas_call(
        functools.partial(kernel, pairs, width, margin, taps.shape[2]),
        out_shape=jax.ShapeDtypeStruct((pairs, 16, width), bf16),
        in_specs=[pl.BlockSpec(memory_space=pl.ANY)]
        + [pl.BlockSpec(memory_space=pltpu.SMEM)] * 3,
        out_specs=pl.BlockSpec(memory_space=pltpu.VMEM),
        scratch_shapes=[
            vmem((planes, rows, width), bf16),
            vmem((2, rows, width), bf16),
            vmem((blocks, 2 * rows, LANES), bf16),
            vmem((blocks, rows, LANES), bf16),
            vmem((blocks, rows // 2, LANES), bf16),
            vmem((3, 2, WINDOW, BLOCK), bf16),
            vmem((pairs, rows, width), bf16),
            vmem((pairs, rows, width), bf16),
            vmem((pairs, rows, width), bf16),
            vmem((2, rows // 2, width), bf16),
            vmem((2, rows // 2, width), bf16),
            vmem((pairs, rows // 2, width), bf16),
            vmem((pairs, rows // 2, width), bf16),
            vmem((pairs, rows // 2, width), bf16),
            vmem((2, rows // 4, width), bf16),
            vmem((2, rows // 4, width), bf16),
            vmem((pairs, rows // 4, width), bf16),
            vmem((pairs, rows // 4, width), bf16),
            vmem((pairs, rows // 4, width), bf16),
            dma((pairs,)),
            dma((pairs,)),
            dma((pairs,)),
            dma((pairs,)),
            dma((pairs,)),
            dma((pairs,)),
            dma((pairs,)),
            dma((3, 2)),
            dma((3, 2)),
        ],
        compiler_params=pltpu.CompilerParams(
            collective_id=0, has_side_effects=True, vmem_limit_bytes=58 * 1024 * 1024
        ),
        cost_estimate=pl.CostEstimate(
            flops=15_000_000_000, bytes_accessed=9 * 1024 * 1024, transcendentals=0
        ),
    )(view_blocks.reshape(planes, rows, width), shifts, taps, ztaps)
    return result.reshape(1, planes, 8, width)


def solution(mesh):
    return jax.shard_map(
        shards,
        mesh=mesh,
        in_specs=(P("views", "slab", None, None), P(), P(), P()),
        out_specs=P("views", "slab", None, None),
        check_vma=False,
    )
```

time: 229 us -> 82.8 us (0.36)
  other arithmetic: 85.1 us -> 0 us
  waiting for transfers between devices: 79.3 us -> 0 us
  Pallas kernels: 0 us -> 77.4 us
  starting transfers between devices: 27.1 us -> 0 us
  between operations: 17.6 us -> 0.01 us
  local copies, waits for them, and re-layouts: 18.7 us -> 5.04 us
    ppermute x9 -> x0, waiting for transfers between devices: 79.3 us -> none  [the longest x3 73.6 us: swapped(): return lax.ppermute(value, axis, pairs)]
    pallas_call x0 -> x1, Pallas kernels: none -> 77.4 us  [shards(): pl.pallas_call(functools.partial(kernel, pairs, width, margin, taps.shape...]
    convert_element_type x6 -> x0, other arithmetic: 56.2 us -> none  [the longest x3 45.8 us: transform(): return total.astype(jnp.bfloat16)]
    add x3 -> x0, other arithmetic: 27.5 us -> none  [transform(): zmix = zmix + zweights[2] * padded[:, 2:].astype(jnp.float32)]
    ppermute x9 -> x0, starting transfers between devices: 27.1 us -> none  [the longest x3 11.9 us: extended(): lax.ppermute(tail, axis, [(i, (i + 1) % count) for i in range(ends)])]
    slice x12 -> x0, local copies, waits for them, and re-layouts: 7.09 us -> none  [the longest x3 1.8 us: transform(): cweights[tap_index] * lax.dynamic_slice_in_dim(wide, start, width, 3)]
    dynamic_slice x7 -> x0, local copies, waits for them, and re-layouts: 4.46 us -> none  [the longest x3 4.16 us: shards(): sent = lax.dynamic_slice_in_dim(interp, send_start, half, 2)]
    unnamed x6 -> x3, local copies, waits for them, and re-layouts: 7.15 us -> 5.04 us
  transfers between devices with their start and end apart: 9 -> 0, of which waited for: 5 -> 0; matrix products, arithmetic and copies ran while one was open for 3% -> 0% of each run, Pallas kernels for 0% -> 0%
where the time goes in v1:
time: 82.8 us; the launch traced here: 82.5 us
  Pallas kernels  77.4 us (93%)
  local copies, waits for them, and re-layouts  5.04 us (6%)
    pallas_call x1, Pallas kernels, shards(): pl.pallas_call(functools.partial(kernel, pairs, width, margin, taps.shape...  77.4 us
    unnamed x3, local copies, waits for them, and re-layouts  5.04 us

profile of v1, /device:TPU:0, one launch (start us, length us, event | category | flops | bytes accessed | tf_op | source)
XLA Modules:
  0.0 82.5 jit_solution(1827415158289971635)
XLA Ops:
  0.0 1.4 %copy.5.taps = f32[3,8,4]{2,1,0:T(8,128)} copy(f32[3,8,4]{1,2,0:T(4,128)} %param.6) | data formatting | bytes 768 | tf_op args[2]
  1.4 1.4 %copy.6.ztaps = f32[3,8,3]{2,1,0:T(8,128)} copy(f32[3,8,3]{1,2,0:T(4,128)} %param.7) | data formatting | bytes 576 | tf_op args[3]
  2.8 77.4 %shard_map.46 = bf16[8,16,4096]{2,1,0:T(8,128)(2,1)} custom-call(bf16[16,64,4096]{2,1,0:T(8,128)(2,1)} %bitcast.3, s32[3,8]{1,0:T(4,128)} %shifts.1, f32[3,8,4]{2,1,0:T(8,128)} %copy.5.taps, f32[3,8,3]{2,1,0:T(8,128)} %copy.6.ztaps), custom_call_target="tpu_custom_call" | custom-call | flops 15000000512 | bytes 9437184 | tf_op jit(solution)/shard_map/pallas_call | solution.py:369
  80.2 2.3 %copy.8 = bf16[1,16,8,4096]{3,2,1,0:T(8,128)(2,1)} copy(bf16[1,16,8,4096]{3,2,1,0:T(8,128)(2,1)} %bitcast.2) | data formatting | bytes 2097152

commit v2 on v1

--- a/solution.py
+++ b/solution.py
@@ -40,6 +40,9 @@
     r1,
     h2s,
     h2r,
+    y1,
+    h3s,
+    h3r,
     k2,
     s2,
     r2,
@@ -61,10 +64,14 @@
     bit1 = (view // 2) % 2
     bit2 = (view // 4) % 2
     core_peer = view + 1 - 2 * bit0
-    peer1 = view + 2 - 4 * bit1
-    peer2 = view + 4 - 8 * bit2
-    first = bit1
-    second = bit2
+    near = view + 2 - 4 * bit1
+    far = view + 4 - 8 * bit2
+    peer1 = near + bit0 * (far - near)
+    peer2 = far + bit0 * (near - far)
+    first = bit1 + bit0 * (bit2 - bit1)
+    second = bit2 + bit0 * (bit1 - bit2)
+    even_core = bit0 == 0
+    odd_core = bit0 == 1
     below = jnp.maximum(slab - 1, 0)
     above = jnp.minimum(slab + 1, last_slab)
     has_below = slab > 0
@@ -115,6 +122,7 @@
     halo0 = halo(0, x_hbm.at[0], x_hbm.at[planes - 1], h0)
     halo1 = halo(1, h1s.at[0], h1s.at[1], h1r)
     halo2 = halo(2, h2s.at[0], h2s.at[1], h2r)
+    halo3 = halo(3, h3s.at[0], h3s.at[1], h3r)
     when_do(has_below, halo0[0].start)
     when_do(has_above, halo0[1].start)
 
@@ -127,7 +135,7 @@
         def _():
             landing[1] = jnp.zeros(landing.shape[1:], landing.dtype)
 
-    for landing in (h0, h1r, h2r):
+    for landing in (h0, h1r, h2r, h3r):
         zero_ends(landing)
 
     edge_blocks = margin // LANES
@@ -139,6 +147,11 @@
 
     groups = [view, view // 2, view // 4]
     bases = []
+    scales = []
+    candidates = 1.0 + (
+        lax.broadcasted_iota(jnp.int32, (8, LANES), 0) * LANES
+        + lax.broadcasted_iota(jnp.int32, (8, LANES), 1)
+    ).astype(jnp.float32) * (1.0 / (8 * LANES))
     for level in range(3):
         start = shifts[level, groups[level]] + (margin - 1)
         base = lax.div(start, jnp.int32(LANES))
@@ -149,15 +162,22 @@
             - lax.broadcasted_iota(jnp.int32, (WINDOW, BLOCK), 1)
             - offset
         )
+        worst = jnp.zeros((8, LANES), jnp.float32)
+        for k in range(tap_count):
+            tap = taps[level, groups[level], k]
+            exact = tap * candidates
+            missed = jnp.abs(exact.astype(jnp.bfloat16).astype(jnp.float32) - exact)
+            worst = jnp.maximum(worst, missed / jnp.maximum(exact, 1e-30))
+        chosen = jnp.where(worst == jnp.min(worst), candidates, 0.0)
+        scale = jnp.max(chosen)
+        scales.append(1.0 / scale)
         values = jnp.zeros((WINDOW, BLOCK), jnp.float32)
         for k in range(tap_count):
-            values = jnp.where(distance == k, 0.5 * taps[level, groups[level], k], values)
-        coarse = values.astype(jnp.bfloat16)
-        band[level, 0] = coarse
-        band[level, 1] = (values - coarse.astype(jnp.float32)).astype(jnp.bfloat16)
+            values = jnp.where(distance == k, taps[level, groups[level], k] * scale, values)
+        band[level] = (0.5 * values).astype(jnp.bfloat16)
 
     def weights(level):
-        return [ztaps[level, groups[level], i] for i in range(3)]
+        return [ztaps[level, groups[level], i] * scales[level] for i in range(3)]
 
     def strips(body):
         def step(i, carry):
@@ -173,7 +193,7 @@
         value = jnp.concatenate([lower, upper], 0).astype(jnp.bfloat16)
         at = lax.div(col, LANES) + edge_blocks
         for i in range(STRIP // LANES):
-            mixes[level][at + i, row : row + 16, :] = value[:, i * LANES : (i + 1) * LANES]
+            mixes[level][at + i, pl.ds(row, 16), :] = value[:, i * LANES : (i + 1) * LANES]
 
     def mix_first(p):
         w = weights(0)
@@ -190,12 +210,18 @@
                     d = f32(h0[1, rows, cols] if p == pairs - 1 else xin[2 * p + 2, rows, cols])
                     lower = w[0] * a + w[1] * b + w[2] * c
                     upper = w[0] * b + w[1] * c + w[2] * d
-                    put(0, 64 * part + 32 * i, col, lower[:8], upper[:8])
-                    put(0, 64 * part + 32 * i + 16, col, lower[8:], upper[8:])
+                    slots = (0, 1 + side) if i == 0 else (2 - side, 3)
+                    for half in range(2):
+                        row = pl.multiple_of(64 * part + 16 * slots[half], 16)
+                        put(
+                            0, row, col,
+                            lower[8 * half : 8 * half + 8],
+                            upper[8 * half : 8 * half + 8],
+                        )
 
         strips(body)
 
-    def mix_later(level, p, source, landing, chunk_starts):
+    def mix_later(level, p, target, source, landing, chunk_starts):
         w = weights(level)
 
         def body(col):
@@ -219,14 +245,15 @@
                 d = edge(1) if p == pairs - 1 else f32(source[p + 1, rows, cols])[:8]
                 lower = w[0] * a + w[1] * b + w[2] * c
                 upper = w[0] * b + w[1] * c + w[2] * d
-                put(level, 16 * at, col, lower, upper)
+                put(target, 16 * at, col, lower, upper)
 
         strips(body)
 
-    def interpolate(level, p, rows, kept, sent):
+    def interpolate(level, p, target, kept, sent):
+        mixed = mixes[target]
+        rows = mixed.shape[1]
         together = max(1, 512 // rows)
         base = bases[level]
-        mixed = mixes[level]
         half = rows // 2
 
         def step(group, carry):
@@ -237,8 +264,7 @@
                     jnp.concatenate([mixed[at + i] for i in range(WINDOW // LANES)], 1)
                 )
             operand = jnp.concatenate(windows, 0)
-            total = jnp.dot(operand, band[level, 0], preferred_element_type=jnp.float32)
-            total += jnp.dot(operand, band[level, 1], preferred_element_type=jnp.float32)
+            total = jnp.dot(operand, band[level], preferred_element_type=jnp.float32)
             for j in range(together):
                 cols = pl.ds(pl.multiple_of((group * together + j) * BLOCK, BLOCK), BLOCK)
                 piece = total[j * rows : (j + 1) * rows].astype(jnp.bfloat16)
@@ -269,6 +295,9 @@
     cross0 = exchange(s0, r0, s0_sem, r0_sem, core_peer)
     cross1 = exchange(s1, r1, s1_sem, r1_sem, peer1)
     cross2 = exchange(s2, r2, s2_sem, r2_sem, peer2)
+    sent_rows = pl.ds(pl.multiple_of(16 - 16 * second, 16), 16)
+    kept_rows = pl.ds(pl.multiple_of(16 * second, 16), 16)
+    cross3 = exchange(x2.at[:, sent_rows], r2, s2_sem, r2_sem, peer2)
 
     def send_edges(p, source, ready, copies, chunks):
         for end, at, half in ((0, 0, 0), (1, pairs - 1, 8)):
@@ -305,7 +334,7 @@
             need(q)
         await_halo(p, halo0)
         mix_first(p)
-        interpolate(0, p, 128, x1, s0)
+        interpolate(0, p, 0, x1, s0)
         cross0[p].start()
 
     def merge0(p):
@@ -313,27 +342,52 @@
         add_into(x1, p, x1, r0)
         send_edges(p, x1, h1s, halo1, 4)
 
-    def level1(p):
-        await_halo(p, halo1)
-        own, other = 2 * first, 2 - 2 * first
-        mix_later(1, p, x1, h1r, [own, own + 1, other, other + 1])
-        interpolate(1, p, 64, x2, s1)
+    own, other = 2 * first, 2 - 2 * first
+
+    def level1_even(p):
+        mix_later(1, p, 1, x1, h1r, [own, own + 1, other, other + 1])
+        interpolate(1, p, 1, x2, s1)
         cross1[p].start()
 
-    def merge1(p):
+    def merge1_even(p):
         cross1[p].wait_recv()
         add_into(x2, p, x2, r1)
         send_edges(p, x2, h2s, halo2, 2)
 
-    def level2(p):
+    def level2_even(p):
         await_halo(p, halo2)
-        mix_later(2, p, x2, h2r, [second, 1 - second])
-        interpolate(2, p, 32, k2, s2)
+        mix_later(2, p, 2, x2, h2r, [second, 1 - second])
+        interpolate(2, p, 2, k2, s2)
         cross2[p].start()
 
-    def merge2(p):
+    def merge2_even(p):
         cross2[p].wait_recv()
         add_into(out, p, k2, r2)
+
+    def level1_odd(p):
+        mix_later(1, p, 1, x1, h1r, [0, 1, 2, 3])
+        interpolate(1, p, 1, y1.at[:, 0:32], y1.at[:, 32:64])
+        send_edges(p, y1, h3s, halo3, 4)
+
+    def level2_odd(p):
+        await_halo(p, halo3)
+        mix_later(2, p, 1, y1, h3r, [own, own + 1, other, other + 1])
+        interpolate(2, p, 1, x2, s1)
+        cross1[p].start()
+
+    def merge1_odd(p):
+        cross1[p].wait_recv()
+        add_into(x2, p, x2, r1)
+        cross3[p].start()
+
+    def merge2_odd(p):
+        cross3[p].wait_recv()
+        add_into(out, p, x2.at[:, kept_rows], r2)
+
+    odd_slots = [(t, (t - 2) % pairs) for t in range(5, pairs + 1)]
+    odd_slots += [(t, (t - 3) % pairs) for t in range(pairs + 2, pairs + 6)]
+    odd_order = dict(odd_slots)
+    odd_list = [p for _, p in odd_slots]
 
     for t in range(pairs + 3):
         if t < pairs:
@@ -341,19 +395,56 @@
         if 1 <= t <= pairs:
             merge0(t % pairs)
         if t >= 3:
-            level1((t - 1) % pairs)
-    for t in range(pairs + 3):
-        if t < pairs:
-            merge1((t + 2) % pairs)
-        if 2 <= t < pairs + 2:
-            level2((t + 1) % pairs)
-        if 3 <= t:
-            merge2(t % pairs)
-
-    for copies in (cross0, cross1, cross2):
+            p = (t - 1) % pairs
+            await_halo(p, halo1)
+
+            @pl.when(even_core)
+            def _():
+                level1_even(p)
+
+            @pl.when(odd_core)
+            def _():
+                level1_odd(p)
+                if t in odd_order:
+                    level2_odd(odd_order[t])
+                    at = odd_list.index(odd_order[t])
+                    if at >= 2:
+                        merge1_odd(odd_list[at - 2])
+
+    @pl.when(even_core)
+    def _():
+        for t in range(pairs + 3):
+            if t < pairs:
+                merge1_even((t + 2) % pairs)
+            if 2 <= t < pairs + 2:
+                level2_even((t + 1) % pairs)
+            if 3 <= t:
+                merge2_even(t % pairs)
+        for p in range(pairs):
+            cross2[p].wait_send()
+        when_do(has_below, halo2[0].wait_send)
+        when_do(has_above, halo2[1].wait_send)
+
+    @pl.when(odd_core)
+    def _():
+        begun = sum(1 for t, _ in odd_slots if t < pairs + 3)
+        for at in range(begun, pairs + 2):
+            if at < pairs:
+                level2_odd(odd_list[at])
+            merge1_odd(odd_list[at - 2])
+            if at - begun >= 1:
+                merge2_odd(odd_list[at - begun - 1])
+        for at in range(pairs + 1 - begun, pairs):
+            merge2_odd(odd_list[at])
+        for p in range(pairs):
+            cross3[p].wait_send()
+        when_do(has_below, halo3[0].wait_send)
+        when_do(has_above, halo3[1].wait_send)
+
+    for copies in (cross0, cross1):
         for copy in copies:
             copy.wait_send()
-    for copies in (halo0, halo1, halo2):
+    for copies in (halo0, halo1):
         when_do(has_below, copies[0].wait_send)
         when_do(has_above, copies[1].wait_send)
 
@@ -378,7 +469,7 @@
             vmem((blocks, 2 * rows, LANES), bf16),
             vmem((blocks, rows, LANES), bf16),
             vmem((blocks, rows // 2, LANES), bf16),
-            vmem((3, 2, WINDOW, BLOCK), bf16),
+            vmem((3, WINDOW, BLOCK), bf16),
             vmem((pairs, rows, width), bf16),
             vmem((pairs, rows, width), bf16),
             vmem((pairs, rows, width), bf16),
@@ -389,6 +480,9 @@
             vmem((pairs, rows // 2, width), bf16),
             vmem((2, rows // 4, width), bf16),
             vmem((2, rows // 4, width), bf16),
+            vmem((pairs, rows, width), bf16),
+            vmem((2, rows // 2, width), bf16),
+            vmem((2, rows // 2, width), bf16),
             vmem((pairs, rows // 4, width), bf16),
             vmem((pairs, rows // 4, width), bf16),
             vmem((pairs, rows // 4, width), bf16),
@@ -399,8 +493,8 @@
             dma((pairs,)),
             dma((pairs,)),
             dma((pairs,)),
-            dma((3, 2)),
-            dma((3, 2)),
+            dma((4, 2)),
+            dma((4, 2)),
         ],
         compiler_params=pltpu.CompilerParams(
             collective_id=0, has_side_effects=True, vmem_limit_bytes=58 * 1024 * 1024

time: 82.8 us -> 75.6 us (0.913)
  Pallas kernels: 77.4 us -> 70.2 us
    pallas_call x1, Pallas kernels: 77.4 us -> 70.2 us  [shards(): pl.pallas_call(functools.partial(kernel, pairs, width, margin, taps.shape...]
where the time goes in v2:
time: 75.6 us; the launch traced here: 75.2 us
  Pallas kernels  70.2 us (93%)
  local copies, waits for them, and re-layouts  5.04 us (7%)
    pallas_call x1, Pallas kernels, shards(): pl.pallas_call(functools.partial(kernel, pairs, width, margin, taps.shape...  70.2 us
    unnamed x3, local copies, waits for them, and re-layouts  5.04 us

profile of v2, /device:TPU:0, one launch (start us, length us, event | category | flops | bytes accessed | tf_op | source)
XLA Modules:
  0.0 75.2 jit_solution(6903503684749317299)
XLA Ops:
  0.0 1.4 %copy.5.taps = f32[3,8,4]{2,1,0:T(8,128)} copy(f32[3,8,4]{1,2,0:T(4,128)} %param.6) | data formatting | bytes 768 | tf_op args[2]
  1.4 1.4 %copy.6.ztaps = f32[3,8,3]{2,1,0:T(8,128)} copy(f32[3,8,3]{1,2,0:T(4,128)} %param.7) | data formatting | bytes 576 | tf_op args[3]
  2.8 70.2 %shard_map.46 = bf16[8,16,4096]{2,1,0:T(8,128)(2,1)} custom-call(bf16[16,64,4096]{2,1,0:T(8,128)(2,1)} %bitcast.3, s32[3,8]{1,0:T(4,128)} %shifts.1, f32[3,8,4]{2,1,0:T(8,128)} %copy.5.taps, f32[3,8,3]{2,1,0:T(8,128)} %copy.6.ztaps), custom_call_target="tpu_custom_call" | custom-call | flops 15000000512 | bytes 9437184 | tf_op jit(solution)/shard_map/pallas_call | solution.py:460
  72.9 2.3 %copy.8 = bf16[1,16,8,4096]{3,2,1,0:T(8,128)(2,1)} copy(bf16[1,16,8,4096]{3,2,1,0:T(8,128)(2,1)} %bitcast.2) | data formatting | bytes 2097152

commit v3 on v2

--- a/solution.py
+++ b/solution.py
@@ -164,7 +164,7 @@
         )
         worst = jnp.zeros((8, LANES), jnp.float32)
         for k in range(tap_count):
-            tap = taps[level, groups[level], k]
+            tap = taps[level, groups[level] * tap_count + k]
             exact = tap * candidates
             missed = jnp.abs(exact.astype(jnp.bfloat16).astype(jnp.float32) - exact)
             worst = jnp.maximum(worst, missed / jnp.maximum(exact, 1e-30))
@@ -173,18 +173,18 @@
         scales.append(1.0 / scale)
         values = jnp.zeros((WINDOW, BLOCK), jnp.float32)
         for k in range(tap_count):
-            values = jnp.where(distance == k, taps[level, groups[level], k] * scale, values)
+            values = jnp.where(distance == k, taps[level, groups[level] * tap_count + k] * scale, values)
         band[level] = (0.5 * values).astype(jnp.bfloat16)
 
     def weights(level):
-        return [ztaps[level, groups[level], i] * scales[level] for i in range(3)]
+        return [ztaps[level, groups[level] * 3 + i] * scales[level] for i in range(3)]
 
     def strips(body):
         def step(i, carry):
             body(pl.multiple_of(i * STRIP, STRIP))
             return carry
 
-        lax.fori_loop(0, width // STRIP, step, 0)
+        lax.fori_loop(0, width // STRIP, step, 0, unroll=2)
 
     def f32(value):
         return value.astype(jnp.float32)
@@ -272,7 +272,7 @@
                 sent[p, :, cols] = piece[half:]
             return carry
 
-        lax.fori_loop(0, width // (BLOCK * together), step, 0)
+        lax.fori_loop(0, width // (BLOCK * together), step, 0, unroll=2 if level < 2 else 1)
 
     def add_into(target, p, kept, received):
         def body(col):
@@ -384,42 +384,75 @@
         cross3[p].wait_recv()
         add_into(out, p, x2.at[:, kept_rows], r2)
 
-    odd_slots = [(t, (t - 2) % pairs) for t in range(5, pairs + 1)]
-    odd_slots += [(t, (t - 3) % pairs) for t in range(pairs + 2, pairs + 6)]
-    odd_order = dict(odd_slots)
-    odd_list = [p for _, p in odd_slots]
-
-    for t in range(pairs + 3):
+    final = pairs - 1
+    late_inner = list(range(3, pairs - 2))
+    odd_early = {5: late_inner[0], 7: late_inner[1]}
+
+    def run(steps):
+        for action, p in steps:
+            action(p)
+
+    def run_even(steps):
+        @pl.when(even_core)
+        def _():
+            run(steps)
+
+    def run_odd(steps):
+        @pl.when(odd_core)
+        def _():
+            run(steps)
+
+    for t in range(pairs + 1):
         if t < pairs:
             level0((t + 1) % pairs)
-        if 1 <= t <= pairs:
+        if t >= 1:
             merge0(t % pairs)
         if t >= 3:
-            p = (t - 1) % pairs
-            await_halo(p, halo1)
-
-            @pl.when(even_core)
-            def _():
-                level1_even(p)
-
-            @pl.when(odd_core)
-            def _():
-                level1_odd(p)
-                if t in odd_order:
-                    level2_odd(odd_order[t])
-                    at = odd_list.index(odd_order[t])
-                    if at >= 2:
-                        merge1_odd(odd_list[at - 2])
+            p = t - 1 if t < pairs else 1
+            run_even([(level1_even, p)])
+            run_odd([(level1_odd, p)])
+        if t in odd_early:
+            run_odd([(level2_odd, odd_early[t])])
+
+    arrivals = list(range(2, pairs - 1)) + [1, final, 0]
+    run_even([(merge1_even, p) for p in arrivals[:3]] + [(level2_even, 3)])
+    run_odd(
+        [(level2_odd, p) for p in late_inner[2:] + [2]] + [(merge1_odd, late_inner[0])]
+    )
+    for p in (final, 0):
+        await_halo(p, halo1)
+        run_even([(level1_even, p)])
+        run_odd([(level1_odd, p)])
+
+    even_steps = []
+    for p in arrivals[3:]:
+        even_steps.append((merge1_even, p))
+        if 5 <= p < final:
+            even_steps.append((level2_even, p - 1))
+        if p == 1:
+            even_steps.append((level2_even, 2))
+            even_steps.append((merge2_even, 3))
+        if p == final:
+            even_steps.append((level2_even, final - 1))
+            even_steps.append((merge2_even, 4))
+    even_steps.append((level2_even, 1))
+    even_steps += [(merge2_even, p) for p in list(range(5, final - 1)) + [2]]
+    even_steps += [(level2_even, final), (level2_even, 0)]
+    even_steps += [(merge2_even, p) for p in (final - 1, 1, final, 0)]
+
+    odd_inner = late_inner + [2]
+    odd_steps = [(level2_odd, final - 1), (level2_odd, 1)]
+    odd_steps += [(merge1_odd, p) for p in odd_inner[1:]]
+    odd_steps += [(merge2_odd, p) for p in odd_inner[:2]]
+    odd_steps += [(level2_odd, final), (level2_odd, 0)]
+    odd_steps += [(merge1_odd, final - 1), (merge1_odd, 1)]
+    odd_steps += [(merge2_odd, p) for p in odd_inner[2:]]
+    odd_steps += [(merge1_odd, final), (merge1_odd, 0)]
+    odd_steps += [(merge2_odd, p) for p in (final - 1, 1, final, 0)]
 
     @pl.when(even_core)
     def _():
-        for t in range(pairs + 3):
-            if t < pairs:
-                merge1_even((t + 2) % pairs)
-            if 2 <= t < pairs + 2:
-                level2_even((t + 1) % pairs)
-            if 3 <= t:
-                merge2_even(t % pairs)
+        run(even_steps)
         for p in range(pairs):
             cross2[p].wait_send()
         when_do(has_below, halo2[0].wait_send)
@@ -427,15 +460,7 @@
 
     @pl.when(odd_core)
     def _():
-        begun = sum(1 for t, _ in odd_slots if t < pairs + 3)
-        for at in range(begun, pairs + 2):
-            if at < pairs:
-                level2_odd(odd_list[at])
-            merge1_odd(odd_list[at - 2])
-            if at - begun >= 1:
-                merge2_odd(odd_list[at - begun - 1])
-        for at in range(pairs + 1 - begun, pairs):
-            merge2_odd(odd_list[at])
+        run(odd_steps)
         for p in range(pairs):
             cross3[p].wait_send()
         when_do(has_below, halo3[0].wait_send)
@@ -502,7 +527,7 @@
         cost_estimate=pl.CostEstimate(
             flops=15_000_000_000, bytes_accessed=9 * 1024 * 1024, transcendentals=0
         ),
-    )(view_blocks.reshape(planes, rows, width), shifts, taps, ztaps)
+    )(view_blocks.reshape(planes, rows, width), shifts, taps.reshape(taps.shape[0], -1), ztaps.reshape(ztaps.shape[0], -1))
     return result.reshape(1, planes, 8, width)
 
 

time: 75.6 us -> 68.4 us (0.905)
  the two profiles are of different devices: /device:TPU:0 before, /device:TPU:1 now
where the time goes in v3:
time: 68.4 us; the launch traced here: 68.1 us
  Pallas kernels  62.9 us (92%)
  local copies, waits for them, and re-layouts  5.17 us (8%)
    pallas_call x1, Pallas kernels, shards(): pl.pallas_call(functools.partial(kernel, pairs, width, margin, taps.shape...  62.9 us
    unnamed x3, local copies, waits for them, and re-layouts  3.84 us

profile of v3, /device:TPU:1, one launch (start us, length us, event | category | flops | bytes accessed | tf_op | source)
XLA Modules:
  0.0 68.1 jit_solution(2337655148046220798)
XLA Ops:
  0.0 0.8 %copy.7 = f32[3,8,4]{2,1,0:T(8,128)S(1)} copy(f32[3,8,4]{1,2,0:T(4,128)} %param.6) | data formatting | bytes 768 | tf_op args[2]
  0.8 0.7 reshape.13.taps
  1.4 0.8 %copy.8 = f32[3,8,3]{2,1,0:T(8,128)S(1)} copy(f32[3,8,3]{1,2,0:T(4,128)} %param.7) | data formatting | bytes 576 | tf_op args[3]
  2.2 0.7 reshape.14.ztaps
  2.9 62.9 %shard_map.46 = bf16[8,16,4096]{2,1,0:T(8,128)(2,1)} custom-call(bf16[16,64,4096]{2,1,0:T(8,128)(2,1)} %bitcast.3, s32[3,8]{1,0:T(4,128)} %shifts.1, f32[3,32]{1,0:T(4,128)} %reshape.13.taps, f32[3,24]{1,0:T(4,128)} %reshape.14.ztaps), custom_call_target="tpu_custom_call" | custom-call | flops 15000000512 | bytes 9437184 | tf_op jit(solution)/shard_map/pallas_call | solution.py:485
  65.8 2.3 %copy.10 = bf16[1,16,8,4096]{3,2,1,0:T(8,128)(2,1)} copy(bf16[1,16,8,4096]{3,2,1,0:T(8,128)(2,1)} %bitcast.2) | data formatting | bytes 2097152
